TPU v7x, 32 devices: a whole 2x2x4 slice. The times are simulated.
32 devices in a mesh: chan: 4 (over z), tm: 8 (over y, x, core).
Axes of the slice: x: 2, y: 2, z: 4, core: 2. Of those that a mesh axis runs over, the one named last changes fastest.
Arguments:
- strain_rate: float32 [1024, 4096], P('chan', 'tm'), may hold values from -64 to 64
Outputs:
- stacks: float32 [32, 2, 13056], P('chan', None, 'tm')
All inputs are finite; a program needn't handle non-finite values.
Results may differ from a plain program's by a relative error of at most 0.0041.
Values may be sent and summed in bfloat16 or wider, within the bound.
No kernel may reach another device: no remote copies, remote signals or barrier semaphores. Data moves between devices by JAX's collectives and lax.ppermute only.
A program may use at most 64 MiB of HBM per device.

v0:
```python
import functools
import math

import jax
import jax.numpy as jnp
from jax import lax
from jax.experimental import pallas as pl
from jax.experimental.pallas import tpu as pltpu
from jax.sharding import PartitionSpec as P

SRC = 8
MAXLAG = 25
W2 = 64
LAGS = 51
FINE = 8
COARSE = -(-LAGS // FINE)
LANES = 128
PAD = 128
CORES = 2


def passed_along(block, axis, distance):
    devices = range(lax.axis_size(axis))
    route = [((i - distance) % len(devices), i) for i in devices]
    return lax.ppermute(block, axis, route)


def band_matrix(rows, columns, related):
    p = lax.broadcasted_iota(jnp.int32, (rows, columns), 0)
    t = lax.broadcasted_iota(jnp.int32, (rows, columns), 1)
    return jnp.where(related(p, t), 1.0, 0.0).astype(jnp.bfloat16)


def halves(values):
    high = values.astype(jnp.bfloat16).astype(jnp.float32)
    return high, values - high


def banded_sums(pieces, band):
    height = pieces[0].shape[0]
    parts = [halves(piece) for piece in pieces]
    stacked = jnp.concatenate([p[0] for p in parts] + [p[1] for p in parts], axis=0)
    sums = jnp.dot(
        stacked.astype(jnp.bfloat16), band, preferred_element_type=jnp.float32
    )
    count = len(pieces)
    return [
        sums[c * height : (c + 1) * height]
        + sums[(count + c) * height : (count + c + 1) * height]
        for c in range(count)
    ]


def level(window_sums):
    return window_sums / (2 * W2 + 1) + 1e-05


def rows_for_here(ref, group, chips):
    me = lax.axis_index("tm")
    every = ref.shape[0] // SRC
    pieces = []
    for m in range(chips):
        start = pl.multiple_of((me ^ (CORES * m)) * group, group)
        pieces.append(ref[pl.ds(start, group)])
    pieces += [ref[q * every : q * every + 1] for q in range(SRC)]
    return jnp.concatenate(pieces, axis=0)


def pack_kernel(group, chips, x_ref, out_ref):
    out_ref[...] = rows_for_here(x_ref, group, chips)


def code_kernel(group, own_ref, other_ref, *outs):
    blocks, sources_ref = outs[:-1], outs[-1]
    first_core = lax.rem(lax.axis_index("tm"), CORES) == 0
    own = own_ref[...]
    other = rows_for_here(other_ref, group, len(blocks))
    x = jnp.concatenate(
        [jnp.where(first_core, own, other), jnp.where(first_core, other, own)], axis=1
    )
    height, length = x.shape
    border = jnp.zeros((height, LANES), jnp.float32)
    magnitude = jnp.concatenate([border, jnp.abs(x), border], axis=1)
    inner = min(256, length)
    band = band_matrix(
        inner + 2 * LANES, inner, lambda p, t: jnp.abs(p - LANES - t) <= W2
    )
    sums = jnp.concatenate(
        banded_sums(
            [
                magnitude[:, start : start + inner + 2 * LANES]
                for start in range(0, length, inner)
            ],
            band,
        ),
        axis=1,
    )
    levels = level(sums)
    normed = x / levels
    left = lax.broadcasted_iota(jnp.int32, (height, LANES), 1) < W2
    tail = length - LANES
    ends = jnp.where(left, normed[:, :LANES], normed[:, tail:])
    end_levels = jnp.where(left, levels[:, :LANES], levels[:, tail:])
    coded = jnp.concatenate([normed, halves(ends)[1], end_levels], axis=1)
    coded = coded.astype(jnp.bfloat16)
    for m, block in enumerate(blocks):
        block[...] = coded[m * group : (m + 1) * group]
    sources_ref[...] = coded[len(blocks) * group :]


def finished_shards(runs, held):
    chips, height, width = held.shape
    length = width - 2 * LANES
    chip = lax.div(lax.axis_index("tm"), CORES)
    for m in range(chips):
        held[chip ^ m] = runs[m]
    left = lax.broadcasted_iota(jnp.int32, (height, LANES), 1) < W2
    tail = length - LANES
    end_values, end_levels = [], []
    for c in range(chips):
        end_values.append(
            jnp.where(left, held[c, :, :LANES], held[c, :, tail:length])
            + held[c, :, length : length + LANES]
        )
        end_levels.append(held[c, :, length + LANES :])

    def meeting(ends, outside):
        outside = [jnp.full((height, LANES), outside, jnp.float32)]
        return [
            jnp.where(left, after, before)
            for before, after in zip(outside + ends, ends + outside)
        ]

    def across(p, t):
        at_p, at_t = jnp.where(p < W2, p, p - LANES), jnp.where(t < W2, t, t - LANES)
        return ((p < W2) != (t < W2)) & (jnp.abs(at_p - at_t) <= W2)

    values, levels = meeting(end_values, 0.0), meeting(end_levels, 1.0)
    added = banded_sums(
        [jnp.abs(v) * l for v, l in zip(values, levels)],
        band_matrix(LANES, LANES, across),
    )
    ends = [
        v * l / (l + a / (2 * W2 + 1)) for v, l, a in zip(values, levels, added)
    ]
    shard = length // CORES
    padding = jnp.zeros((height, PAD), jnp.float32)
    for k in range(chips * CORES):
        c, part = k // CORES, k % CORES
        pieces = [held[c, :, part * shard : (part + 1) * shard], padding]
        if part == 0:
            head = jnp.where(left, ends[c], held[c, :, :LANES])
            pieces = [head, held[c, :, LANES:shard], padding]
        if part == CORES - 1:
            last = jnp.where(left, held[c, :, tail:length], ends[c + 1])
            pieces = [held[c, :, part * shard : tail], last, padding]
        yield jnp.concatenate(pieces, axis=1)


def receiver_kernel(group, *refs):
    *blocks, out_ref, held = refs
    runs = [ref[...].astype(jnp.float32)[:group] for ref in blocks]
    for k, wide in enumerate(finished_shards(runs, held)):
        fine = [pltpu.roll(wide, MAXLAG - j, 1) for j in range(FINE)]
        out_ref[k] = jnp.concatenate(fine, axis=0).astype(jnp.bfloat16)


def correlate_kernel(offsets, scale, receivers_ref, own_ref, other_ref, *refs):
    outs, (held, mixed, table) = refs[:offsets], refs[offsets:]
    chips, sources = held.shape[:2]
    group = receivers_ref.shape[1] // FINE
    first_core = lax.rem(lax.axis_index("tm"), CORES) == 0
    own, other = [ref[...].astype(jnp.float32) for ref in (own_ref, other_ref)]
    high, low = jnp.where(first_core, own, other), jnp.where(first_core, other, own)
    half = sources // CORES
    runs = [
        jnp.concatenate(
            [low[m * half : (m + 1) * half], high[m * half : (m + 1) * half]], axis=0
        )
        for m in range(chips)
    ]
    product = None
    for k, wide in enumerate(finished_shards(runs, held)):
        coarse = [pltpu.roll(wide, FINE * i, 1) if i else wide for i in range(COARSE)]
        term = lax.dot_general(
            receivers_ref[k],
            jnp.concatenate(coarse, axis=0).astype(jnp.bfloat16),
            (((1,), (1,)), ((), ())),
            preferred_element_type=jnp.float32,
        )
        product = term if product is None else product + term
    product = product * scale
    for h in range(mixed.shape[0]):
        first, last = h * LANES, min((h + 1) * LANES, COARSE * sources)
        for j in range(FINE):
            mixed[h, pl.ds(j, group, stride=FINE), : last - first] = product[
                j * group : (j + 1) * group, first:last
            ]
        table[h * LANES : (h + 1) * LANES] = mixed[h].T
    lane = lax.broadcasted_iota(jnp.int32, (sources, LANES), 1)
    width = group * LAGS
    tiles = [None] * -(-width // LANES)

    def place(tile, piece, low, high):
        if tiles[tile] is None:
            tiles[tile] = piece
        elif low == 0:
            tiles[tile] = jnp.where(lane < high, piece, tiles[tile])
        else:
            tiles[tile] = jnp.where(lane >= low, piece, tiles[tile])

    for b in range(group):
        column = b * FINE
        for i in range(COARSE):
            piece = table[
                i * sources : (i + 1) * sources,
                column // LANES * LANES : (column // LANES + 1) * LANES,
            ]
            start = b * LAGS + i * FINE
            shift = (start - column) % LANES
            if shift:
                piece = pltpu.roll(piece, shift, 1)
            count = min(FINE, LAGS - i * FINE)
            tile, low = start // LANES, start % LANES
            place(tile, piece, low, LANES)
            if low + count > LANES:
                tiles[tile + 1] = piece
    for tile, value in enumerate(tiles):
        first = tile * LANES
        last = min(first + LANES, width)
        for o in range(offsets):
            rows = value[o * SRC : (o + 1) * SRC, : last - first]
            outs[o][:, first:last] = rows.astype(jnp.bfloat16)


def stack_kernel(*refs):
    out_ref = refs[-1]
    for o, ref in enumerate(refs[:-1]):
        out_ref[:, o, :] = ref[...].astype(jnp.float32)


def call(kernel, out_shape, inputs, scratch=(), flops=0):
    single = not isinstance(out_shape, list)
    spec = pl.BlockSpec(memory_space=pltpu.VMEM)
    moved = sum(v.size * v.dtype.itemsize for v in inputs)
    return pl.pallas_call(
        kernel,
        out_shape=out_shape,
        in_specs=[spec] * len(inputs),
        out_specs=spec if single else [spec] * len(out_shape),
        scratch_shapes=list(scratch),
        compiler_params=pltpu.CompilerParams(vmem_limit_bytes=32 * 1024 * 1024),
        cost_estimate=pl.CostEstimate(
            flops=flops, bytes_accessed=moved, transcendentals=0
        ),
    )(*inputs)


def swapped(block, axis, m):
    devices = range(lax.axis_size(axis))
    return lax.ppermute(block, axis, [(k, k ^ m) for k in devices])


def from_blocks(block, first, second):
    count, places = lax.axis_size("chan"), lax.axis_size("tm")
    route = []
    for i in range(count):
        for k in range(places):
            d = first if k % CORES == 0 else second
            route.append((((i - d) % count) * places + k, i * places + k))
    return lax.ppermute(block, ("chan", "tm"), route)


def body(strain_rate):
    channels, length = strain_rate.shape
    shards = lax.axis_size("tm")
    chips = shards // CORES
    reach = lax.axis_size("chan") // 4
    group = channels // shards
    steps = list(range(-reach, 0)) + list(range(1, reach + 1))
    offsets = len(steps)
    sources = offsets * SRC
    scale = 1.0 / math.sqrt(length * shards)
    run = CORES * length
    coded = run + 2 * LANES

    other = swapped(strain_rate, "tm", 1)
    own = call(
        functools.partial(pack_kernel, group, chips),
        jax.ShapeDtypeStruct((chips * group + SRC, length), jnp.float32),
        [strain_rate],
        flops=8 * channels * length,
    )
    *blocks, own_sources = call(
        functools.partial(code_kernel, group),
        [jax.ShapeDtypeStruct((group, coded), jnp.bfloat16)] * chips
        + [jax.ShapeDtypeStruct((SRC, coded), jnp.bfloat16)],
        [own, other],
        flops=8 * (chips * group + SRC) * run * (256 + 2 * LANES),
    )
    arrived = [from_blocks(own_sources, steps[reach + h], steps[h]) for h in range(reach)]
    blocks = [jnp.concatenate([block] + arrived) for block in blocks]
    blocks = blocks[:1] + [swapped(blocks[m], "tm", CORES * m) for m in range(1, chips)]
    own = jnp.concatenate([block[group:] for block in blocks])
    other = swapped(own, "tm", 1)
    receivers = call(
        functools.partial(receiver_kernel, group),
        jax.ShapeDtypeStruct((shards, FINE * group, length + PAD), jnp.bfloat16),
        blocks,
        scratch=[pltpu.VMEM((chips, group, coded), jnp.float32)],
        flops=shards * group * 2 * length * length,
    )
    columns = -(-group * FINE // LANES) * LANES
    heights = -(-COARSE * sources // LANES) * LANES
    results = call(
        functools.partial(correlate_kernel, offsets, scale),
        [jax.ShapeDtypeStruct((SRC, group * LAGS), jnp.bfloat16)] * offsets,
        [receivers, own, other],
        scratch=[
            pltpu.VMEM((chips, sources, coded), jnp.float32),
            pltpu.VMEM((heights // LANES, columns, LANES), jnp.float32),
            pltpu.VMEM((heights, columns), jnp.float32),
        ],
        flops=2 * shards * (length + PAD) * group * FINE * COARSE * sources,
    )
    arrived = [passed_along(r, "chan", -d) for r, d in zip(results, steps)]
    return call(
        stack_kernel,
        jax.ShapeDtypeStruct((SRC, offsets, group * LAGS), jnp.float32),
        arrived,
    )


def solution(mesh):
    placed = (P("chan", "tm"),)
    return jax.shard_map(
        body, mesh=mesh, in_specs=placed, out_specs=P("chan", None, "tm"), check_vma=False
    )
```

profile of v0, /device:TPU:0, one launch (start us, length us, event | category | flops | bytes accessed | tf_op | source)
XLA Modules:
  0.0 27.0 jit_solution(4333940296375464090)
XLA Ops:
  0.0 0.5 %collective-permute-start = (f32[256,512]{1,0:T(8,128)}, f32[256,512]{1,0:T(8,128)S(1)}, u32[]{:S(2)}, u32[]{:S(2)}) collective-permute-start(f32[256,512]{1,0:T(8,128)} %x_ref.1), channel_id=1, source_target_pairs={{0,1},{1,0},{2,3},{3,2},{4,5},{5,4},{6,7},{7,6},{8,9},{9,8},{10,11... | collective-permute-start | bytes 1572872 | tf_op jit(solution)/shard_map/ppermute | solution.py:261
  0.5 0.0 copy-start
  0.5 1.0 %copy-done = f32[256,512]{1,0:T(8,128)S(1)} copy-done((f32[256,512]{1,0:T(8,128)S(1)}, f32[256,512]{1,0:T(8,128)}, u32[]{:S(2)}) %copy-start) | copy-done | bytes 524312
  1.5 0.7 %collective-permute-done.other_ref = f32[256,512]{1,0:T(8,128)S(1)} collective-permute-done((f32[256,512]{1,0:T(8,128)}, f32[256,512]{1,0:T(8,128)S(1)}, u32[]{:S(2)}, u32[]{:S(2)}) %collective-permute-start) | collective-permute-done | bytes 524320 | tf_op jit(solution)/shard_map/ppermute | solution.py:261
  2.2 0.5 %shard_map.18 = (bf16[32,1280]{1,0:T(8,128)(2,1)S(1)}, bf16[32,1280]{1,0:T(8,128)(2,1)S(1)}, bf16[32,1280]{1,0:T(8,128)(2,1)S(1)}, bf16[32,1280]{1,0:T(8,128)(2,1)S(1)}, bf16[8,1280]{1,0:T(8,128)(2,1)S(1)}) custom-call(f32[136,512]{1,0:T(8,128)S(1)} %shard_map.17.own_ref, f32[256,512]{1,0:T(8,128)S(1)} %collective-permute-done.other_ref), custom_call_target="tpu_custom_call" | custom-call | flops 570425344 | bytes 802816 | tf_op jit(solution)/shard_map/pallas_call | solution.py:246
  2.7 3.0 %collective-permute-start.1 = (bf16[8,1280]{1,0:T(8,128)(2,1)S(1)}, bf16[8,1280]{1,0:T(8,128)(2,1)S(1)}, u32[]{:S(2)}, u32[]{:S(2)}) collective-permute-start(bf16[8,1280]{1,0:T(8,128)(2,1)S(1)} %get-tuple-element.13), channel_id=1, source_target_pairs={{24,0},{9,1},{26,2},{11,3},{28,4},{13,5},{30,6},{15,7},{0,8},{17,9... | collective-permute-start | bytes 61448 | tf_op jit(solution)/shard_map/ppermute | solution.py:271
  5.7 3.8 %collective-permute-done.1 = bf16[8,1280]{1,0:T(8,128)(2,1)S(1)} collective-permute-done((bf16[8,1280]{1,0:T(8,128)(2,1)S(1)}, bf16[8,1280]{1,0:T(8,128)(2,1)S(1)}, u32[]{:S(2)}, u32[]{:S(2)}) %collective-permute-start.1) | collective-permute-done | bytes 20512 | tf_op jit(solution)/shard_map/ppermute | solution.py:271
  9.5 2.7 %collective-permute-start.4 = (bf16[40,1280]{1,0:T(8,128)(2,1)S(1)}, bf16[40,1280]{1,0:T(8,128)(2,1)S(1)}, u32[]{:S(2)}, u32[]{:S(2)}) collective-permute-start(bf16[40,1280]{1,0:T(8,128)(2,1)S(1)} %get-tuple-element.19), channel_id=1, source_target_pairs={{0,6},{1,7},{2,4},{3,5},{4,2},{5,3},{6,0},{7,1},{8,14},{9,15},{10,... | collective-permute-start | bytes 307208 | tf_op jit(solution)/shard_map/ppermute | solution.py:261
  12.3 0.5 %collective-permute-start.3 = (bf16[40,1280]{1,0:T(8,128)(2,1)S(1)}, bf16[40,1280]{1,0:T(8,128)(2,1)S(1)}, u32[]{:S(2)}, u32[]{:S(2)}) collective-permute-start(bf16[40,1280]{1,0:T(8,128)(2,1)S(1)} %get-tuple-element.21), channel_id=1, source_target_pairs={{0,4},{1,5},{2,6},{3,7},{4,0},{5,1},{6,2},{7,3},{8,12},{9,13},{10,... | collective-permute-start | bytes 307208 | tf_op jit(solution)/shard_map/ppermute | solution.py:261
  12.8 0.3 %collective-permute-start.2 = (bf16[40,1280]{1,0:T(8,128)(2,1)S(1)}, bf16[40,1280]{1,0:T(8,128)(2,1)S(1)}, u32[]{:S(2)}, u32[]{:S(2)}) collective-permute-start(bf16[40,1280]{1,0:T(8,128)(2,1)S(1)} %get-tuple-element.20), channel_id=1, source_target_pairs={{0,2},{1,3},{2,0},{3,1},{4,6},{5,7},{6,4},{7,5},{8,10},{9,11},{10,... | collective-permute-start | bytes 307208 | tf_op jit(solution)/shard_map/ppermute | solution.py:261
  13.1 2.8 %collective-permute-done.4.refs_3_ = bf16[40,1280]{1,0:T(8,128)(2,1)S(1)} collective-permute-done((bf16[40,1280]{1,0:T(8,128)(2,1)S(1)}, bf16[40,1280]{1,0:T(8,128)(2,1)S(1)}, u32[]{:S(2)}, u32[]{:S(2)}) %collective-permute-start.4) | collective-permute-done | bytes 102432 | tf_op jit(solution)/shard_map/ppermute | solution.py:261
  15.8 1.1 %collective-permute-done.3.refs_2_ = bf16[40,1280]{1,0:T(8,128)(2,1)S(1)} collective-permute-done((bf16[40,1280]{1,0:T(8,128)(2,1)S(1)}, bf16[40,1280]{1,0:T(8,128)(2,1)S(1)}, u32[]{:S(2)}, u32[]{:S(2)}) %collective-permute-start.3) | collective-permute-done | bytes 102432 | tf_op jit(solution)/shard_map/ppermute | solution.py:261
  16.9 0.5 %collective-permute-done.2.refs_1_ = bf16[40,1280]{1,0:T(8,128)(2,1)S(1)} collective-permute-done((bf16[40,1280]{1,0:T(8,128)(2,1)S(1)}, bf16[40,1280]{1,0:T(8,128)(2,1)S(1)}, u32[]{:S(2)}, u32[]{:S(2)}) %collective-permute-start.2) | collective-permute-done | bytes 102432 | tf_op jit(solution)/shard_map/ppermute | solution.py:261
  17.4 0.1 collective-permute-start.5
  17.5 0.7 %shard_map.19.receivers_ref = bf16[8,256,640]{2,1,0:T(8,128)(2,1)S(1)} custom-call(bf16[40,1280]{1,0:T(8,128)(2,1)S(1)} %get-tuple-element.22.refs_0_, bf16[40,1280]{1,0:T(8,128)(2,1)S(1)} %collective-permute-done.2.refs_1_, bf16[40,1280]{1,0:T(8,128)(2,1)S(1)} %collective-permute-done.3.refs_2_, bf16[40,1280]{1,0:T(8,128)(2,1)S(1)} %collective-permute-done.4.refs_3_), custom_call_target="tpu_custom_call" | custom-call | flops 134217728 | bytes 409600 | tf_op jit(solution)/shard_map/pallas_call | solution.py:246
  18.2 0.5 %collective-permute-done.5.other_ref = bf16[32,1280]{1,0:T(8,128)(2,1)S(1)} collective-permute-done((bf16[32,1280]{1,0:T(8,128)(2,1)S(1)}, bf16[32,1280]{1,0:T(8,128)(2,1)S(1)}, u32[]{:S(2)}, u32[]{:S(2)}) %collective-permute-start.5) | collective-permute-done | bytes 81952 | tf_op jit(solution)/shard_map/ppermute | solution.py:261
  18.8 1.6 %shard_map.20 = (bf16[8,1632]{1,0:T(8,128)(2,1)S(1)}, bf16[8,1632]{1,0:T(8,128)(2,1)S(1)}) custom-call(bf16[8,256,640]{2,1,0:T(8,128)(2,1)S(1)} %shard_map.19.receivers_ref, bf16[32,1280]{1,0:T(8,128)(2,1)S(1)} %pad_maximum_fusion.4.own_ref, bf16[32,1280]{1,0:T(8,128)(2,1)S(1)} %collective-permute-done.5.other_ref), custom_call_target="tpu_custom_call" | custom-call | flops 293601280 | bytes 2785280 | tf_op jit(solution)/shard_map/pallas_call | solution.py:246
  20.4 0.1 collective-permute-start.6
  20.4 3.8 %collective-permute-start.7 = (bf16[8,1632]{1,0:T(8,128)(2,1)S(1)}, bf16[8,1632]{1,0:T(8,128)(2,1)S(1)}, u32[]{:S(2)}, u32[]{:S(2)}) collective-permute-start(bf16[8,1632]{1,0:T(8,128)(2,1)S(1)} %get-tuple-element.18), channel_id=1, source_target_pairs={{8,0},{16,8},{24,16},{0,24},{9,1},{17,9},{25,17},{1,25},{10,2},{18... | collective-permute-start | bytes 78344 | tf_op jit(solution)/shard_map/ppermute | solution.py:25
  24.2 2.1 %collective-permute-done.6.refs_0_ = bf16[8,1632]{1,0:T(8,128)(2,1)S(1)} collective-permute-done((bf16[8,1632]{1,0:T(8,128)(2,1)S(1)}, bf16[8,1632]{1,0:T(8,128)(2,1)S(1)}, u32[]{:S(2)}, u32[]{:S(2)}) %collective-permute-start.6) | collective-permute-done | bytes 26144 | tf_op jit(solution)/shard_map/ppermute | solution.py:25
  26.3 0.0 collective-permute-done.7.refs_1_
  26.3 0.7 %shard_map.21 = f32[8,2,1632]{2,1,0:T(2,128)} custom-call(bf16[8,1632]{1,0:T(8,128)(2,1)S(1)} %collective-permute-done.6.refs_0_, bf16[8,1632]{1,0:T(8,128)(2,1)S(1)} %collective-permute-done.7.refs_1_), custom_call_target="tpu_custom_call" | custom-call | bytes 52224 | tf_op jit(solution)/shard_map/pallas_call | solution.py:246
  (6 shorter events, 0.1 us)
Async XLA Ops:
  0.0 2.2 %collective-permute-start = (f32[256,512]{1,0:T(8,128)}, f32[256,512]{1,0:T(8,128)S(1)}, u32[]{:S(2)}, u32[]{:S(2)}) collective-permute-start(f32[256,512]{1,0:T(8,128)} %x_ref.1), channel_id=1, source_target_pairs={{0,1},{1,0},{2,3},{3,2},{4,5},{5,4},{6,7},{7,6},{8,9},{9,8},{10,11... | collective-permute-start | bytes 1572872 | tf_op jit(solution)/shard_map/ppermute | solution.py:261
  0.5 1.0 %copy-start = (f32[256,512]{1,0:T(8,128)S(1)}, f32[256,512]{1,0:T(8,128)}, u32[]{:S(2)}) copy-start(f32[256,512]{1,0:T(8,128)} %x_ref.1) | copy-start | bytes 1572868
  2.7 6.8 %collective-permute-start.1 = (bf16[8,1280]{1,0:T(8,128)(2,1)S(1)}, bf16[8,1280]{1,0:T(8,128)(2,1)S(1)}, u32[]{:S(2)}, u32[]{:S(2)}) collective-permute-start(bf16[8,1280]{1,0:T(8,128)(2,1)S(1)} %get-tuple-element.13), channel_id=1, source_target_pairs={{24,0},{9,1},{26,2},{11,3},{28,4},{13,5},{30,6},{15,7},{0,8},{17,9... | collective-permute-start | bytes 61448 | tf_op jit(solution)/shard_map/ppermute | solution.py:271
  9.5 6.3 %collective-permute-start.4 = (bf16[40,1280]{1,0:T(8,128)(2,1)S(1)}, bf16[40,1280]{1,0:T(8,128)(2,1)S(1)}, u32[]{:S(2)}, u32[]{:S(2)}) collective-permute-start(bf16[40,1280]{1,0:T(8,128)(2,1)S(1)} %get-tuple-element.19), channel_id=1, source_target_pairs={{0,6},{1,7},{2,4},{3,5},{4,2},{5,3},{6,0},{7,1},{8,14},{9,15},{10,... | collective-permute-start | bytes 307208 | tf_op jit(solution)/shard_map/ppermute | solution.py:261
  12.3 4.7 %collective-permute-start.3 = (bf16[40,1280]{1,0:T(8,128)(2,1)S(1)}, bf16[40,1280]{1,0:T(8,128)(2,1)S(1)}, u32[]{:S(2)}, u32[]{:S(2)}) collective-permute-start(bf16[40,1280]{1,0:T(8,128)(2,1)S(1)} %get-tuple-element.21), channel_id=1, source_target_pairs={{0,4},{1,5},{2,6},{3,7},{4,0},{5,1},{6,2},{7,3},{8,12},{9,13},{10,... | collective-permute-start | bytes 307208 | tf_op jit(solution)/shard_map/ppermute | solution.py:261
  12.8 4.7 %collective-permute-start.2 = (bf16[40,1280]{1,0:T(8,128)(2,1)S(1)}, bf16[40,1280]{1,0:T(8,128)(2,1)S(1)}, u32[]{:S(2)}, u32[]{:S(2)}) collective-permute-start(bf16[40,1280]{1,0:T(8,128)(2,1)S(1)} %get-tuple-element.20), channel_id=1, source_target_pairs={{0,2},{1,3},{2,0},{3,1},{4,6},{5,7},{6,4},{7,5},{8,10},{9,11},{10,... | collective-permute-start | bytes 307208 | tf_op jit(solution)/shard_map/ppermute | solution.py:261
  17.4 1.3 %collective-permute-start.5 = (bf16[32,1280]{1,0:T(8,128)(2,1)S(1)}, bf16[32,1280]{1,0:T(8,128)(2,1)S(1)}, u32[]{:S(2)}, u32[]{:S(2)}) collective-permute-start(bf16[32,1280]{1,0:T(8,128)(2,1)S(1)} %pad_maximum_fusion.4.own_ref), channel_id=1, source_target_pairs={{0,1},{1,0},{2,3},{3,2},{4,5},{5,4},{6,7},{7,6},{8,9},{9,8},{10,11... | collective-permute-start | bytes 245768 | tf_op jit(solution)/shard_map/ppermute | solution.py:261
  20.4 5.9 %collective-permute-start.6 = (bf16[8,1632]{1,0:T(8,128)(2,1)S(1)}, bf16[8,1632]{1,0:T(8,128)(2,1)S(1)}, u32[]{:S(2)}, u32[]{:S(2)}) collective-permute-start(bf16[8,1632]{1,0:T(8,128)(2,1)S(1)} %get-tuple-element.17), channel_id=1, source_target_pairs={{24,0},{0,8},{8,16},{16,24},{25,1},{1,9},{9,17},{17,25},{26,2},{2,... | collective-permute-start | bytes 78344 | tf_op jit(solution)/shard_map/ppermute | solution.py:25
  20.4 5.9 %collective-permute-start.7 = (bf16[8,1632]{1,0:T(8,128)(2,1)S(1)}, bf16[8,1632]{1,0:T(8,128)(2,1)S(1)}, u32[]{:S(2)}, u32[]{:S(2)}) collective-permute-start(bf16[8,1632]{1,0:T(8,128)(2,1)S(1)} %get-tuple-element.18), channel_id=1, source_target_pairs={{8,0},{16,8},{24,16},{0,24},{9,1},{17,9},{25,17},{1,25},{10,2},{18... | collective-permute-start | bytes 78344 | tf_op jit(solution)/shard_map/ppermute | solution.py:25
where the time goes:
time: 27.1 us; the launch traced here: 27 us
  waiting for transfers between devices  11.4 us (42%)
  starting transfers between devices  10.9 us (40%)
  Pallas kernels  3.5 us (13%)
  local copies, waits for them, and re-layouts  1.05 us (4%)
    ppermute x5, waiting for transfers between devices, swapped(): return lax.ppermute(block, axis, [(k, k ^ m) for k in devices])  5.55 us
    ppermute x5, starting transfers between devices, swapped(): return lax.ppermute(block, axis, [(k, k ^ m) for k in devices])  4.08 us
    ppermute x2, starting transfers between devices, passed_along(): return lax.ppermute(block, axis, route)  3.87 us
    ppermute x1, waiting for transfers between devices, from_blocks(): return lax.ppermute(block, ('chan', 'tm'), route)  3.78 us
    pallas_call x5, Pallas kernels, call(): pl.pallas_call(kernel, out_shape=out_shape, in_specs=[spec] * len(inputs)...  3.5 us
    ppermute x1, starting transfers between devices, from_blocks(): return lax.ppermute(block, ('chan', 'tm'), route)  3 us
    ppermute x2, waiting for transfers between devices, passed_along(): return lax.ppermute(block, axis, route)  2.06 us
    unnamed x2, local copies, waits for them, and re-layouts  1.04 us
  transfers between devices with their start and end apart: 8, of which 7 were waited for; matrix products, arithmetic and copies ran while one was open for 0% of the time, Pallas kernels for 3%

commit v1 on v0

--- a/solution.py
+++ b/solution.py
@@ -70,11 +70,8 @@
     out_ref[...] = rows_for_here(x_ref, group, chips)
 
 
-def code_kernel(group, own_ref, other_ref, *outs):
-    blocks, sources_ref = outs[:-1], outs[-1]
+def coded_rows(own, other):
     first_core = lax.rem(lax.axis_index("tm"), CORES) == 0
-    own = own_ref[...]
-    other = rows_for_here(other_ref, group, len(blocks))
     x = jnp.concatenate(
         [jnp.where(first_core, own, other), jnp.where(first_core, other, own)], axis=1
     )
@@ -102,10 +99,29 @@
     ends = jnp.where(left, normed[:, :LANES], normed[:, tail:])
     end_levels = jnp.where(left, levels[:, :LANES], levels[:, tail:])
     coded = jnp.concatenate([normed, halves(ends)[1], end_levels], axis=1)
-    coded = coded.astype(jnp.bfloat16)
+    return coded.astype(jnp.bfloat16)
+
+
+def code_sources_kernel(group, chips, own_ref, other_ref, out_ref):
+    first = chips * group
+    other = rows_for_here(other_ref, group, chips)
+    out_ref[...] = coded_rows(own_ref[first:], other[first:])
+
+
+def code_receivers_kernel(group, chips, own_ref, other_ref, out_ref):
+    last = chips * group
+    other = rows_for_here(other_ref, group, chips)
+    out_ref[...] = coded_rows(own_ref[:last], other[:last])
+
+
+def join_kernel(offsets, receivers_ref, *refs):
+    given, blocks = refs[:offsets], refs[offsets:]
+    group = receivers_ref.shape[0] // len(blocks)
+    sources = [ref[...].astype(jnp.float32) for ref in given]
+    receivers = receivers_ref[...].astype(jnp.float32)
     for m, block in enumerate(blocks):
-        block[...] = coded[m * group : (m + 1) * group]
-    sources_ref[...] = coded[len(blocks) * group :]
+        rows = [receivers[m * group : (m + 1) * group]] + sources
+        block[...] = jnp.concatenate(rows, axis=0).astype(jnp.bfloat16)
 
 
 def finished_shards(runs, held):
@@ -157,33 +173,22 @@
         yield jnp.concatenate(pieces, axis=1)
 
 
-def receiver_kernel(group, *refs):
-    *blocks, out_ref, held = refs
-    runs = [ref[...].astype(jnp.float32)[:group] for ref in blocks]
-    for k, wide in enumerate(finished_shards(runs, held)):
-        fine = [pltpu.roll(wide, MAXLAG - j, 1) for j in range(FINE)]
-        out_ref[k] = jnp.concatenate(fine, axis=0).astype(jnp.bfloat16)
-
-
-def correlate_kernel(offsets, scale, receivers_ref, own_ref, other_ref, *refs):
+def correlate_kernel(offsets, scale, *refs):
+    chips = len(refs) - offsets - 3
+    blocks, refs = refs[:chips], refs[chips:]
     outs, (held, mixed, table) = refs[:offsets], refs[offsets:]
-    chips, sources = held.shape[:2]
-    group = receivers_ref.shape[1] // FINE
-    first_core = lax.rem(lax.axis_index("tm"), CORES) == 0
-    own, other = [ref[...].astype(jnp.float32) for ref in (own_ref, other_ref)]
-    high, low = jnp.where(first_core, own, other), jnp.where(first_core, other, own)
-    half = sources // CORES
-    runs = [
-        jnp.concatenate(
-            [low[m * half : (m + 1) * half], high[m * half : (m + 1) * half]], axis=0
-        )
-        for m in range(chips)
-    ]
+    sources = offsets * SRC
+    group = held.shape[1] - sources
+    runs = [ref[...].astype(jnp.float32) for ref in blocks[:1] + blocks[:0:-1]]
     product = None
-    for k, wide in enumerate(finished_shards(runs, held)):
-        coarse = [pltpu.roll(wide, FINE * i, 1) if i else wide for i in range(COARSE)]
+    for wide in finished_shards(runs, held):
+        receivers, senders = wide[:group], wide[group:]
+        fine = [pltpu.roll(receivers, MAXLAG - j, 1) for j in range(FINE)]
+        coarse = [
+            pltpu.roll(senders, FINE * i, 1) if i else senders for i in range(COARSE)
+        ]
         term = lax.dot_general(
-            receivers_ref[k],
+            jnp.concatenate(fine, axis=0).astype(jnp.bfloat16),
             jnp.concatenate(coarse, axis=0).astype(jnp.bfloat16),
             (((1,), (1,)), ((), ())),
             preferred_element_type=jnp.float32,
@@ -261,16 +266,6 @@
     return lax.ppermute(block, axis, [(k, k ^ m) for k in devices])
 
 
-def from_blocks(block, first, second):
-    count, places = lax.axis_size("chan"), lax.axis_size("tm")
-    route = []
-    for i in range(count):
-        for k in range(places):
-            d = first if k % CORES == 0 else second
-            route.append((((i - d) % count) * places + k, i * places + k))
-    return lax.ppermute(block, ("chan", "tm"), route)
-
-
 def body(strain_rate):
     channels, length = strain_rate.shape
     shards = lax.axis_size("tm")
@@ -291,33 +286,34 @@
         [strain_rate],
         flops=8 * channels * length,
     )
-    *blocks, own_sources = call(
-        functools.partial(code_kernel, group),
-        [jax.ShapeDtypeStruct((group, coded), jnp.bfloat16)] * chips
-        + [jax.ShapeDtypeStruct((SRC, coded), jnp.bfloat16)],
+    own_sources = call(
+        functools.partial(code_sources_kernel, group, chips),
+        jax.ShapeDtypeStruct((SRC, coded), jnp.bfloat16),
         [own, other],
-        flops=8 * (chips * group + SRC) * run * (256 + 2 * LANES),
-    )
-    arrived = [from_blocks(own_sources, steps[reach + h], steps[h]) for h in range(reach)]
-    blocks = [jnp.concatenate([block] + arrived) for block in blocks]
-    blocks = blocks[:1] + [swapped(blocks[m], "tm", CORES * m) for m in range(1, chips)]
-    own = jnp.concatenate([block[group:] for block in blocks])
-    other = swapped(own, "tm", 1)
-    receivers = call(
-        functools.partial(receiver_kernel, group),
-        jax.ShapeDtypeStruct((shards, FINE * group, length + PAD), jnp.bfloat16),
-        blocks,
-        scratch=[pltpu.VMEM((chips, group, coded), jnp.float32)],
-        flops=shards * group * 2 * length * length,
-    )
+    )
+    arrived = [passed_along(own_sources, "chan", d) for d in steps]
+    own_receivers = call(
+        functools.partial(code_receivers_kernel, group, chips),
+        jax.ShapeDtypeStruct((chips * group, coded), jnp.bfloat16),
+        [own, other],
+        flops=8 * chips * group * run * (256 + 2 * LANES),
+    )
+    blocks = call(
+        functools.partial(join_kernel, offsets),
+        [jax.ShapeDtypeStruct((group + sources, coded), jnp.bfloat16)] * chips,
+        [own_receivers] + arrived,
+    )
+    blocks = list(blocks[:1]) + [
+        swapped(blocks[m], "tm", CORES * m) for m in range(chips - 1, 0, -1)
+    ]
     columns = -(-group * FINE // LANES) * LANES
     heights = -(-COARSE * sources // LANES) * LANES
     results = call(
         functools.partial(correlate_kernel, offsets, scale),
         [jax.ShapeDtypeStruct((SRC, group * LAGS), jnp.bfloat16)] * offsets,
-        [receivers, own, other],
+        blocks,
         scratch=[
-            pltpu.VMEM((chips, sources, coded), jnp.float32),
+            pltpu.VMEM((chips, group + sources, coded), jnp.float32),
             pltpu.VMEM((heights // LANES, columns, LANES), jnp.float32),
             pltpu.VMEM((heights, columns), jnp.float32),
         ],

time: 27.1 us -> 25.9 us (0.956)
  waiting for transfers between devices: 11.4 us -> 8.43 us
  starting transfers between devices: 10.9 us -> 13 us
    ppermute x2 -> x4, starting transfers between devices: 3.87 us -> 8.96 us  [passed_along(): return lax.ppermute(block, axis, route)]
    ppermute x1 -> x0, waiting for transfers between devices: 3.78 us -> none  [from_blocks(): return lax.ppermute(block, ('chan', 'tm'), route)]
    ppermute x1 -> x0, starting transfers between devices: 3 us -> none  [from_blocks(): return lax.ppermute(block, ('chan', 'tm'), route)]
    ppermute x2 -> x4, waiting for transfers between devices: 2.06 us -> 3.26 us  [passed_along(): return lax.ppermute(block, axis, route)]
    ppermute x5 -> x4, waiting for transfers between devices: 5.55 us -> 5.18 us  [swapped(): return lax.ppermute(block, axis, [(k, k ^ m) for k in devices])]
    pallas_call x5 -> x6, Pallas kernels: 3.5 us -> 3.24 us  [call(): pl.pallas_call(kernel, out_shape=out_shape, in_specs=[spec] * len(inputs)...]
    ppermute x5 -> x4, starting transfers between devices: 4.08 us -> 4.01 us  [swapped(): return lax.ppermute(block, axis, [(k, k ^ m) for k in devices])]
  transfers between devices with their start and end apart: 8 -> 8, of which waited for: 7 -> 7; matrix products, arithmetic and copies ran while one was open for 0% -> 0% of each run, Pallas kernels for 3% -> 2%
where the time goes in v1:
time: 25.9 us; the launch traced here: 25.7 us
  starting transfers between devices  13 us (50%)
  waiting for transfers between devices  8.43 us (33%)
  Pallas kernels  3.24 us (13%)
  local copies, waits for them, and re-layouts  1.04 us (4%)
    ppermute x4, starting transfers between devices, passed_along(): return lax.ppermute(block, axis, route)  8.96 us
    ppermute x4, waiting for transfers between devices, swapped(): return lax.ppermute(block, axis, [(k, k ^ m) for k in devices])  5.18 us
    ppermute x4, starting transfers between devices, swapped(): return lax.ppermute(block, axis, [(k, k ^ m) for k in devices])  4.01 us
    ppermute x4, waiting for transfers between devices, passed_along(): return lax.ppermute(block, axis, route)  3.26 us
    pallas_call x6, Pallas kernels, call(): pl.pallas_call(kernel, out_shape=out_shape, in_specs=[spec] * len(inputs)...  3.24 us
    unnamed x2, local copies, waits for them, and re-layouts  1.04 us
  transfers between devices with their start and end apart: 8, of which 7 were waited for; matrix products, arithmetic and copies ran while one was open for 0% of the time, Pallas kernels for 2%

profile of v1, /device:TPU:0, one launch (start us, length us, event | category | flops | bytes accessed | tf_op | source)
XLA Modules:
  0.0 25.7 jit_solution(10805923366595233452)
XLA Ops:
  0.0 0.5 %collective-permute-start = (f32[256,512]{1,0:T(8,128)}, f32[256,512]{1,0:T(8,128)S(1)}, u32[]{:S(2)}, u32[]{:S(2)}) collective-permute-start(f32[256,512]{1,0:T(8,128)} %x_ref.1), channel_id=1, source_target_pairs={{0,1},{1,0},{2,3},{3,2},{4,5},{5,4},{6,7},{7,6},{8,9},{9,8},{10,11... | collective-permute-start | bytes 1572872 | tf_op jit(solution)/shard_map/ppermute | solution.py:266
  0.5 0.0 copy-start
  0.5 1.0 %copy-done = f32[256,512]{1,0:T(8,128)S(1)} copy-done((f32[256,512]{1,0:T(8,128)S(1)}, f32[256,512]{1,0:T(8,128)}, u32[]{:S(2)}) %copy-start) | copy-done | bytes 524312
  1.5 0.7 %collective-permute-done.other_ref = f32[256,512]{1,0:T(8,128)S(1)} collective-permute-done((f32[256,512]{1,0:T(8,128)}, f32[256,512]{1,0:T(8,128)S(1)}, u32[]{:S(2)}, u32[]{:S(2)}) %collective-permute-start) | collective-permute-done | bytes 524320 | tf_op jit(solution)/shard_map/ppermute | solution.py:266
  2.2 0.2 shard_map.19
  2.4 3.0 %collective-permute-start.2 = (bf16[8,1280]{1,0:T(8,128)(2,1)S(1)}, bf16[8,1280]{1,0:T(8,128)(2,1)S(1)}, u32[]{:S(2)}, u32[]{:S(2)}) collective-permute-start(bf16[8,1280]{1,0:T(8,128)(2,1)S(1)} %shard_map.19), channel_id=1, source_target_pairs={{24,0},{0,8},{8,16},{16,24},{25,1},{1,9},{9,17},{17,25},{26,2},{2,... | collective-permute-start | bytes 61448 | tf_op jit(solution)/shard_map/ppermute | solution.py:25
  5.4 2.1 %collective-permute-start.1 = (bf16[8,1280]{1,0:T(8,128)(2,1)S(1)}, bf16[8,1280]{1,0:T(8,128)(2,1)S(1)}, u32[]{:S(2)}, u32[]{:S(2)}) collective-permute-start(bf16[8,1280]{1,0:T(8,128)(2,1)S(1)} %shard_map.19), channel_id=1, source_target_pairs={{8,0},{16,8},{24,16},{0,24},{9,1},{17,9},{25,17},{1,25},{10,2},{18... | collective-permute-start | bytes 61448 | tf_op jit(solution)/shard_map/ppermute | solution.py:25
  7.5 0.5 %shard_map.18.receivers_ref = bf16[128,1280]{1,0:T(8,128)(2,1)S(1)} custom-call(f32[136,512]{1,0:T(8,128)S(1)} %shard_map.17.own_ref, f32[256,512]{1,0:T(8,128)S(1)} %collective-permute-done.other_ref), custom_call_target="tpu_custom_call" | custom-call | flops 536870912 | bytes 802816 | tf_op jit(solution)/shard_map/pallas_call | solution.py:251
  8.0 1.3 %collective-permute-done.2.refs_1_ = bf16[8,1280]{1,0:T(8,128)(2,1)S(1)} collective-permute-done((bf16[8,1280]{1,0:T(8,128)(2,1)S(1)}, bf16[8,1280]{1,0:T(8,128)(2,1)S(1)}, u32[]{:S(2)}, u32[]{:S(2)}) %collective-permute-start.2) | collective-permute-done | bytes 20512 | tf_op jit(solution)/shard_map/ppermute | solution.py:25
  9.3 0.1 collective-permute-done.1.refs_0_
  9.5 2.5 %collective-permute-start.3 = (bf16[48,1280]{1,0:T(8,128)(2,1)S(1)}, bf16[48,1280]{1,0:T(8,128)(2,1)S(1)}, u32[]{:S(2)}, u32[]{:S(2)}) collective-permute-start(bf16[48,1280]{1,0:T(8,128)(2,1)S(1)} %get-tuple-element.12), channel_id=1, source_target_pairs={{0,6},{1,7},{2,4},{3,5},{4,2},{5,3},{6,0},{7,1},{8,14},{9,15},{10,... | collective-permute-start | bytes 368648 | tf_op jit(solution)/shard_map/ppermute | solution.py:266
  12.0 0.5 %collective-permute-start.4 = (bf16[48,1280]{1,0:T(8,128)(2,1)S(1)}, bf16[48,1280]{1,0:T(8,128)(2,1)S(1)}, u32[]{:S(2)}, u32[]{:S(2)}) collective-permute-start(bf16[48,1280]{1,0:T(8,128)(2,1)S(1)} %get-tuple-element.13), channel_id=1, source_target_pairs={{0,4},{1,5},{2,6},{3,7},{4,0},{5,1},{6,2},{7,3},{8,12},{9,13},{10,... | collective-permute-start | bytes 368648 | tf_op jit(solution)/shard_map/ppermute | solution.py:266
  12.5 0.5 %collective-permute-start.5 = (bf16[48,1280]{1,0:T(8,128)(2,1)S(1)}, bf16[48,1280]{1,0:T(8,128)(2,1)S(1)}, u32[]{:S(2)}, u32[]{:S(2)}) collective-permute-start(bf16[48,1280]{1,0:T(8,128)(2,1)S(1)} %get-tuple-element.14), channel_id=1, source_target_pairs={{0,2},{1,3},{2,0},{3,1},{4,6},{5,7},{6,4},{7,5},{8,10},{9,11},{10,... | collective-permute-start | bytes 368648 | tf_op jit(solution)/shard_map/ppermute | solution.py:266
  13.0 3.1 %collective-permute-done.3.refs_1_ = bf16[48,1280]{1,0:T(8,128)(2,1)S(1)} collective-permute-done((bf16[48,1280]{1,0:T(8,128)(2,1)S(1)}, bf16[48,1280]{1,0:T(8,128)(2,1)S(1)}, u32[]{:S(2)}, u32[]{:S(2)}) %collective-permute-start.3) | collective-permute-done | bytes 122912 | tf_op jit(solution)/shard_map/ppermute | solution.py:266
  16.1 1.2 %collective-permute-done.4.refs_2_ = bf16[48,1280]{1,0:T(8,128)(2,1)S(1)} collective-permute-done((bf16[48,1280]{1,0:T(8,128)(2,1)S(1)}, bf16[48,1280]{1,0:T(8,128)(2,1)S(1)}, u32[]{:S(2)}, u32[]{:S(2)}) %collective-permute-start.4) | collective-permute-done | bytes 122912 | tf_op jit(solution)/shard_map/ppermute | solution.py:266
  17.3 0.2 collective-permute-done.5.refs_3_
  17.5 1.8 %shard_map.21 = (bf16[8,1632]{1,0:T(8,128)(2,1)S(1)}, bf16[8,1632]{1,0:T(8,128)(2,1)S(1)}) custom-call(bf16[48,1280]{1,0:T(8,128)(2,1)S(1)} %get-tuple-element.11.refs_0_, bf16[48,1280]{1,0:T(8,128)(2,1)S(1)} %collective-permute-done.3.refs_1_, bf16[48,1280]{1,0:T(8,128)(2,1)S(1)} %collective-permute-done.4.refs_2_, ...), custom_call_target="tpu_custom_call" | custom-call | flops 293601280 | bytes 491520 | tf_op jit(solution)/shard_map/pallas_call | solution.py:251
  19.3 1.3 %collective-permute-start.6 = (bf16[8,1632]{1,0:T(8,128)(2,1)S(1)}, bf16[8,1632]{1,0:T(8,128)(2,1)S(1)}, u32[]{:S(2)}, u32[]{:S(2)}) collective-permute-start(bf16[8,1632]{1,0:T(8,128)(2,1)S(1)} %get-tuple-element.15), channel_id=1, source_target_pairs={{24,0},{0,8},{8,16},{16,24},{25,1},{1,9},{9,17},{17,25},{26,2},{2,... | collective-permute-start | bytes 78344 | tf_op jit(solution)/shard_map/ppermute | solution.py:25
  20.6 2.6 %collective-permute-start.7 = (bf16[8,1632]{1,0:T(8,128)(2,1)S(1)}, bf16[8,1632]{1,0:T(8,128)(2,1)S(1)}, u32[]{:S(2)}, u32[]{:S(2)}) collective-permute-start(bf16[8,1632]{1,0:T(8,128)(2,1)S(1)} %get-tuple-element.16), channel_id=1, source_target_pairs={{8,0},{16,8},{24,16},{0,24},{9,1},{17,9},{25,17},{1,25},{10,2},{18... | collective-permute-start | bytes 78344 | tf_op jit(solution)/shard_map/ppermute | solution.py:25
  23.2 1.8 %collective-permute-done.6.refs_0_ = bf16[8,1632]{1,0:T(8,128)(2,1)S(1)} collective-permute-done((bf16[8,1632]{1,0:T(8,128)(2,1)S(1)}, bf16[8,1632]{1,0:T(8,128)(2,1)S(1)}, u32[]{:S(2)}, u32[]{:S(2)}) %collective-permute-start.6) | collective-permute-done | bytes 26144 | tf_op jit(solution)/shard_map/ppermute | solution.py:25
  25.0 0.0 collective-permute-done.7.refs_1_
  25.0 0.7 %shard_map.22 = f32[8,2,1632]{2,1,0:T(2,128)} custom-call(bf16[8,1632]{1,0:T(8,128)(2,1)S(1)} %collective-permute-done.6.refs_0_, bf16[8,1632]{1,0:T(8,128)(2,1)S(1)} %collective-permute-done.7.refs_1_), custom_call_target="tpu_custom_call" | custom-call | bytes 52224 | tf_op jit(solution)/shard_map/pallas_call | solution.py:251
  (2 shorter events, 0.1 us)
Async XLA Ops:
  0.0 2.2 %collective-permute-start = (f32[256,512]{1,0:T(8,128)}, f32[256,512]{1,0:T(8,128)S(1)}, u32[]{:S(2)}, u32[]{:S(2)}) collective-permute-start(f32[256,512]{1,0:T(8,128)} %x_ref.1), channel_id=1, source_target_pairs={{0,1},{1,0},{2,3},{3,2},{4,5},{5,4},{6,7},{7,6},{8,9},{9,8},{10,11... | collective-permute-start | bytes 1572872 | tf_op jit(solution)/shard_map/ppermute | solution.py:266
  0.5 1.0 %copy-start = (f32[256,512]{1,0:T(8,128)S(1)}, f32[256,512]{1,0:T(8,128)}, u32[]{:S(2)}) copy-start(f32[256,512]{1,0:T(8,128)} %x_ref.1) | copy-start | bytes 1572868
  2.4 6.9 %collective-permute-start.2 = (bf16[8,1280]{1,0:T(8,128)(2,1)S(1)}, bf16[8,1280]{1,0:T(8,128)(2,1)S(1)}, u32[]{:S(2)}, u32[]{:S(2)}) collective-permute-start(bf16[8,1280]{1,0:T(8,128)(2,1)S(1)} %shard_map.19), channel_id=1, source_target_pairs={{24,0},{0,8},{8,16},{16,24},{25,1},{1,9},{9,17},{17,25},{26,2},{2,... | collective-permute-start | bytes 61448 | tf_op jit(solution)/shard_map/ppermute | solution.py:25
  5.4 4.0 %collective-permute-start.1 = (bf16[8,1280]{1,0:T(8,128)(2,1)S(1)}, bf16[8,1280]{1,0:T(8,128)(2,1)S(1)}, u32[]{:S(2)}, u32[]{:S(2)}) collective-permute-start(bf16[8,1280]{1,0:T(8,128)(2,1)S(1)} %shard_map.19), channel_id=1, source_target_pairs={{8,0},{16,8},{24,16},{0,24},{9,1},{17,9},{25,17},{1,25},{10,2},{18... | collective-permute-start | bytes 61448 | tf_op jit(solution)/shard_map/ppermute | solution.py:25
  9.5 6.7 %collective-permute-start.3 = (bf16[48,1280]{1,0:T(8,128)(2,1)S(1)}, bf16[48,1280]{1,0:T(8,128)(2,1)S(1)}, u32[]{:S(2)}, u32[]{:S(2)}) collective-permute-start(bf16[48,1280]{1,0:T(8,128)(2,1)S(1)} %get-tuple-element.12), channel_id=1, source_target_pairs={{0,6},{1,7},{2,4},{3,5},{4,2},{5,3},{6,0},{7,1},{8,14},{9,15},{10,... | collective-permute-start | bytes 368648 | tf_op jit(solution)/shard_map/ppermute | solution.py:266
  12.0 5.4 %collective-permute-start.4 = (bf16[48,1280]{1,0:T(8,128)(2,1)S(1)}, bf16[48,1280]{1,0:T(8,128)(2,1)S(1)}, u32[]{:S(2)}, u32[]{:S(2)}) collective-permute-start(bf16[48,1280]{1,0:T(8,128)(2,1)S(1)} %get-tuple-element.13), channel_id=1, source_target_pairs={{0,4},{1,5},{2,6},{3,7},{4,0},{5,1},{6,2},{7,3},{8,12},{9,13},{10,... | collective-permute-start | bytes 368648 | tf_op jit(solution)/shard_map/ppermute | solution.py:266
  12.5 5.0 %collective-permute-start.5 = (bf16[48,1280]{1,0:T(8,128)(2,1)S(1)}, bf16[48,1280]{1,0:T(8,128)(2,1)S(1)}, u32[]{:S(2)}, u32[]{:S(2)}) collective-permute-start(bf16[48,1280]{1,0:T(8,128)(2,1)S(1)} %get-tuple-element.14), channel_id=1, source_target_pairs={{0,2},{1,3},{2,0},{3,1},{4,6},{5,7},{6,4},{7,5},{8,10},{9,11},{10,... | collective-permute-start | bytes 368648 | tf_op jit(solution)/shard_map/ppermute | solution.py:266
  19.3 5.7 %collective-permute-start.6 = (bf16[8,1632]{1,0:T(8,128)(2,1)S(1)}, bf16[8,1632]{1,0:T(8,128)(2,1)S(1)}, u32[]{:S(2)}, u32[]{:S(2)}) collective-permute-start(bf16[8,1632]{1,0:T(8,128)(2,1)S(1)} %get-tuple-element.15), channel_id=1, source_target_pairs={{24,0},{0,8},{8,16},{16,24},{25,1},{1,9},{9,17},{17,25},{26,2},{2,... | collective-permute-start | bytes 78344 | tf_op jit(solution)/shard_map/ppermute | solution.py:25
  20.6 4.5 %collective-permute-start.7 = (bf16[8,1632]{1,0:T(8,128)(2,1)S(1)}, bf16[8,1632]{1,0:T(8,128)(2,1)S(1)}, u32[]{:S(2)}, u32[]{:S(2)}) collective-permute-start(bf16[8,1632]{1,0:T(8,128)(2,1)S(1)} %get-tuple-element.16), channel_id=1, source_target_pairs={{8,0},{16,8},{24,16},{0,24},{9,1},{17,9},{25,17},{1,25},{10,2},{18... | collective-permute-start | bytes 78344 | tf_op jit(solution)/shard_map/ppermute | solution.py:25
